TPU v7x, 32 devices: a whole 2x2x4 slice. The times are simulated.
32 devices in a mesh: survey: 2 (over x), freq: 16 (over z, y, core).
Axes of the slice: x: 2, y: 2, z: 4, core: 2. Of those that a mesh axis runs over, the one named last changes fastest.
Arguments:
- gathers: float32 [4096, 2048], P(('survey', 'freq')), parts along dimension 0, may hold values from -6 to 6
- operator: bfloat16 [64, 2, 1024, 1024], P(('survey', 'freq')), parts along dimension 0, may hold values from -0.125 to 0.125
- filters: float32 [32, 4, 9, 31], P(('survey', 'freq')), parts along dimension 0, may hold values from -0.18 to 0.18
- tile_of: int32 [32], P('survey'), parts along dimension 0, may hold values from 0 to 15, each once
- slice_len: int32 [32], P('survey'), parts along dimension 0, may hold values from 1 to 2, 20 in all
Outputs:
- primaries: float32 [4096, 2048], P(('survey', 'freq')), parts along dimension 0
There are 2 independent parts, one for each index of `survey`. A program takes and returns all parts, laid end to end along the dimension named above; each array names one. Nothing has to cross between parts.
Inputs may be any that keep to these rules, and one draw needn't show every extreme that they name: `tile_of`: each tile is held by exactly one block of rows. `slice_len`: the entries sum to 20; the largest equals 2.
All inputs are finite; a program needn't handle non-finite values.
Results may differ from a plain program's by a relative error of at most 0.0027.
Values may be sent and summed in bfloat16 or wider, within the bound.
No kernel may reach another device: no remote copies, remote signals or barrier semaphores. Data moves between devices by JAX's collectives and lax.ppermute only.
A program may use at most 64 MiB of HBM per device.

v0:
```python
import functools
import math

import jax
import jax.numpy as jnp
import ml_dtypes
import numpy as np
from jax import lax
from jax.experimental import pallas as pl
from jax.experimental.pallas import tpu as pltpu
from jax.sharding import PartitionSpec as P

FIRST = 40
REACH = 4
VMEM_LIMIT = 40 * 1024 * 1024


def split_halves(values):
    values = values.astype(np.float32)
    high = values.astype(ml_dtypes.bfloat16)
    low = (values - high.astype(np.float32)).astype(ml_dtypes.bfloat16)
    return high, low


def row_tables(band_bins, length):
    bin_ids = FIRST + np.arange(band_bins)
    angles = 2.0 * np.pi / length * (bin_ids[:, None] * np.arange(length)[None, :] % length)
    return np.stack([np.cos(angles), -np.sin(angles)], axis=1).reshape(2 * band_bins, length)


def lag_tables(band_bins, lags, length):
    bin_ids = FIRST + np.arange(band_bins)
    lag_ids = np.arange(lags) - lags // 2
    angles = 2.0 * np.pi / length * (bin_ids[:, None] * lag_ids[None, :] % length)
    cosine, sine = np.cos(angles), np.sin(angles)
    weight = (bin_ids / (FIRST + band_bins))[:, None]
    real = np.stack([cosine, sine, -weight * sine, weight * cosine])
    imag = np.stack([sine, -cosine, weight * cosine, weight * sine])
    own = np.stack([real, real], axis=2).reshape(4, 2 * band_bins, lags)
    partner = np.stack([-imag, imag], axis=2).reshape(4, 2 * band_bins, lags)
    return np.concatenate([own, partner], axis=1).astype(np.float32)


def split_array(values):
    high = values.astype(jnp.bfloat16)
    low = (values - high.astype(jnp.float32)).astype(jnp.bfloat16)
    return high, low


def swap_pairs(values):
    rows = values.shape[0]
    parity = lax.broadcasted_iota(jnp.int32, values.shape, 0) % 2
    return jnp.where(
        parity == 0, pltpu.roll(values, rows - 1, 0), pltpu.roll(values, 1, 0)
    )


def spectrum_kernel(chunk, gathers_ref, table_ref, out_ref, held, table, sems):
    length = gathers_ref.shape[1]
    rows = table_ref.shape[0] // 2
    copies = []
    for step in range(length // chunk):
        part = pl.ds(step * chunk, chunk)
        copies.append(
            (
                pltpu.make_async_copy(gathers_ref.at[:, part], held.at[:, part], sems.at[0, step]),
                pltpu.make_async_copy(table_ref.at[:, part], table.at[:, part], sems.at[1, step]),
            )
        )
    for pair in copies:
        for copy in pair:
            copy.start()
    dot = functools.partial(
        lax.dot_general,
        dimension_numbers=(((1,), (1,)), ((), ())),
        preferred_element_type=jnp.float32,
    )
    total = jnp.zeros((rows, held.shape[0]), jnp.float32)
    for step, pair in enumerate(copies):
        for copy in pair:
            copy.wait()
        part = pl.ds(step * chunk, chunk)
        high, low = split_array(held[:, part])
        weights = table[:, part]
        both = dot(weights, high)
        total = total + both[:rows] + (both[rows:] + dot(weights[:rows], low))
    out_ref[...] = total.astype(jnp.bfloat16).reshape(out_ref.shape)


def fill_coefficients(kept_bins, slots, counts, filters, table, out_ref):
    offsets, components, _ = filters.shape
    _, rows, width = out_ref.shape
    total = jnp.zeros((2 * rows, offsets), jnp.float32)
    for part in range(components):
        total = total + lax.dot_general(
            table[part],
            filters[:, part],
            (((1,), (1,)), ((), ())),
            precision=lax.Precision.HIGHEST,
            preferred_element_type=jnp.float32,
        )
    row_ids = lax.broadcasted_iota(jnp.int32, (rows, width), 0)
    group = row_ids // (2 * slots)
    slot = row_ids // 2 % slots
    count = jnp.zeros((rows, width), jnp.int32)
    for device in range(rows // (2 * slots)):
        count = jnp.where(group == device, counts[device], count)
    scale = jnp.where(slot < count, math.sqrt(2.0 / kept_bins), 0.0)
    for offset in range(offsets):
        out_ref[offset] = total[:rows, offset : offset + 1] * scale
        out_ref[offsets + offset] = total[rows:, offset : offset + 1] * scale


def predict_kernel(
    kept_bins,
    pieces,
    incoming_ref,
    tile_ref,
    slice_ref,
    filters_ref,
    lag_ref,
    operator_ref,
    out_ref,
    coefficient_ref,
    tile_of,
    counts,
    filters,
    lags,
    operator,
    spectra,
    tiles,
    small_sems,
    sems,
):
    devices, group_rows, traces = incoming_ref.shape
    slots, _, receivers, _ = operator_ref.shape
    per_shot = receivers // traces
    shots = devices // per_shot
    rows = shots * group_rows
    span = receivers // pieces
    pairs = ((tile_ref, tile_of), (slice_ref, counts), (filters_ref, filters), (lag_ref, lags))
    small = [
        pltpu.make_async_copy(source, target, small_sems.at[i])
        for i, (source, target) in enumerate(pairs)
    ]
    for copy in small:
        copy.start()
    copies = {}
    for slot in range(slots):
        for piece in range(pieces):
            for part in range(2):
                where = (slot, part, pl.ds(piece * span, span))
                copies[slot, piece, part] = pltpu.make_async_copy(
                    operator_ref.at[where], operator.at[where], sems.at[slot, piece, part]
                )
                copies[slot, piece, part].start()
    for copy in small:
        copy.wait()
    for k in range(devices):
        spectra[tile_of[k]] = incoming_ref[k].astype(jnp.float32)
    columns = []
    for q in range(per_shot):
        parts = [spectra[s * per_shot + q] for s in range(shots)]
        columns.append(jnp.concatenate(parts, axis=0))
    spectrum = jnp.concatenate(columns, axis=1).astype(jnp.bfloat16)
    fill_coefficients(kept_bins, slots, counts, filters, lags, coefficient_ref)
    row_ids = lax.broadcasted_iota(jnp.int32, (rows, span), 0)
    dot = functools.partial(
        lax.dot_general,
        dimension_numbers=(((1,), (1,)), ((), ())),
        preferred_element_type=jnp.float32,
    )
    kept = {}
    for slot in range(slots):
        for piece in range(pieces):
            where = pl.ds(piece * span, span)
            copies[slot, piece, 0].wait()
            by_real = dot(spectrum, operator[slot, 0, where])
            copies[slot, piece, 1].wait()
            by_imag = swap_pairs(dot(spectrum, operator[slot, 1, where]))
            product = jnp.where(row_ids % 2 == 0, by_real - by_imag, by_real + by_imag)
            if slot:
                product = jnp.where(row_ids // 2 % slots == slot, product, kept[piece])
            kept[piece] = product
            if slot == slots - 1:
                for s in range(shots):
                    for q in range(span // traces):
                        tiles[s * per_shot + piece * span // traces + q] = product[
                            s * group_rows : (s + 1) * group_rows, q * traces : (q + 1) * traces
                        ]
    lane_ids = lax.broadcasted_iota(jnp.int32, (group_rows, traces), 1)
    for k in range(devices):
        tile = tile_of[k]
        place = tile % per_shot
        before = tiles[jnp.maximum(tile - 1, 0)]
        after = tiles[jnp.minimum(tile + 1, devices - 1)]
        first_lanes = jnp.where(place < per_shot - 1, REACH, 0)
        last_lanes = jnp.where(place > 0, traces - REACH, traces)
        halo = jnp.where(lane_ids < first_lanes, after, 0.0)
        halo = jnp.where(lane_ids >= last_lanes, before, halo)
        out_ref[k] = jnp.concatenate([tiles[tile], halo], axis=1).astype(jnp.bfloat16)


def subtract_kernel(chunk, returned_ref, coefficient_ref, table_ref, gathers_ref, out_ref, result, sems):
    devices, group_rows, width = returned_ref.shape
    rows = devices * group_rows
    traces, length = gathers_ref.shape
    own = returned_ref[...].astype(jnp.float32).reshape(rows, width)
    partner = swap_pairs(own)
    offsets = coefficient_ref.shape[0] // 2
    total = jnp.zeros((rows, traces), jnp.float32)
    for offset in range(offsets):
        shift = (offsets // 2 - offset) % width
        moved = pltpu.roll(own, shift, 1)[:, :traces]
        moved_partner = pltpu.roll(partner, shift, 1)[:, :traces]
        total = total + coefficient_ref[offset] * moved
        total = total + coefficient_ref[offsets + offset] * moved_partner
    high, low = split_array(jnp.transpose(total))
    stacked = jnp.concatenate([high, low, high], axis=1)
    copies = []
    for step in range(length // chunk):
        part = pl.ds(step * chunk, chunk)
        response = jnp.dot(stacked, table_ref[:, part], preferred_element_type=jnp.float32)
        result[:, part] = gathers_ref[:, part] - response
        copy = pltpu.make_async_copy(result.at[:, part], out_ref.at[:, part], sems.at[step])
        copy.start()
        copies.append(copy)
    for copy in copies:
        copy.wait()


def vmem_spec():
    return pl.BlockSpec(memory_space=pltpu.VMEM)


def hbm_spec():
    return pl.BlockSpec(memory_space=pltpu.HBM)


def in_hbm(values):
    return pltpu.with_memory_space_constraint(values, pltpu.HBM)


def local(gathers, operator, filters, tile_of, slice_len):
    devices = lax.axis_size("freq")
    traces, length = gathers.shape
    slots, _, receivers, _ = operator.shape
    band_bins = slots * devices
    rows = 2 * band_bins
    group_rows = 2 * slots
    kept_bins = 5 * devices // 4
    offsets, lags = filters.shape[2], filters.shape[3]
    chunk = length // 4
    params = pltpu.CompilerParams(vmem_limit_bytes=VMEM_LIMIT)
    table = row_tables(band_bins, length)
    forward_table = np.concatenate(split_halves(table / math.sqrt(length)), axis=0)
    back_high, back_low = split_halves(table)
    back_table = np.concatenate([back_high, back_high, back_low], axis=0)
    with jax.named_scope("spectrum"):
        outgoing = pl.pallas_call(
            functools.partial(spectrum_kernel, chunk),
            out_shape=jax.ShapeDtypeStruct((devices, group_rows, traces), jnp.bfloat16),
            in_specs=[hbm_spec()] * 2,
            out_specs=vmem_spec(),
            scratch_shapes=[
                pltpu.VMEM((traces, length), jnp.float32),
                pltpu.VMEM((2 * rows, length), jnp.bfloat16),
                pltpu.SemaphoreType.DMA((2, length // chunk)),
            ],
            compiler_params=params,
            name="spectrum",
        )(in_hbm(gathers), in_hbm(jnp.asarray(forward_table)))
    incoming = lax.all_to_all(outgoing, "freq", split_axis=0, concat_axis=0, tiled=True)
    with jax.named_scope("predict"):
        tables = lag_tables(band_bins, lags, length)
        pieces = 2
        sending, coefficients = pl.pallas_call(
            functools.partial(predict_kernel, kept_bins, pieces),
            out_shape=[
                jax.ShapeDtypeStruct((devices, group_rows, 2 * traces), jnp.bfloat16),
                jax.ShapeDtypeStruct((2 * offsets, rows, traces), jnp.float32),
            ],
            in_specs=[vmem_spec()] + [hbm_spec()] * 5,
            out_specs=[vmem_spec(), vmem_spec()],
            scratch_shapes=[
                pltpu.SMEM(tile_of.shape, jnp.int32),
                pltpu.SMEM(slice_len.shape, jnp.int32),
                pltpu.VMEM((offsets, filters.shape[1], lags), jnp.float32),
                pltpu.VMEM(tables.shape, jnp.float32),
                pltpu.VMEM(operator.shape, operator.dtype),
                pltpu.VMEM((devices, group_rows, traces), jnp.float32),
                pltpu.VMEM((devices, group_rows, traces), jnp.float32),
                pltpu.SemaphoreType.DMA((4,)),
                pltpu.SemaphoreType.DMA((slots, pieces, 2)),
            ],
            compiler_params=params,
            name="predict",
        )(
            incoming,
            in_hbm(tile_of),
            in_hbm(slice_len),
            in_hbm(jnp.transpose(filters[0], (1, 0, 2))),
            in_hbm(jnp.asarray(tables)),
            in_hbm(operator),
        )
    returned = lax.all_to_all(sending, "freq", split_axis=0, concat_axis=0, tiled=True)
    with jax.named_scope("subtract"):
        return pl.pallas_call(
            functools.partial(subtract_kernel, chunk),
            out_shape=jax.ShapeDtypeStruct((traces, length), jnp.float32),
            in_specs=[vmem_spec()] * 4,
            out_specs=hbm_spec(),
            scratch_shapes=[
                pltpu.VMEM((traces, length), jnp.float32),
                pltpu.SemaphoreType.DMA((length // chunk,)),
            ],
            compiler_params=params,
            name="subtract",
        )(returned, coefficients, jnp.asarray(back_table), gathers)


def solution(mesh):
    placed = (
        P(("survey", "freq"), None),
        P(("survey", "freq"), None, None, None),
        P(("survey", "freq"), None, None, None),
        P("survey"),
        P("survey"),
    )
    return jax.shard_map(
        local, mesh=mesh, in_specs=placed, out_specs=P(("survey", "freq"), None), check_vma=False
    )
```

profile of v0, /device:TPU:0, one launch (start us, length us, event | category | flops | bytes accessed | tf_op | source)
XLA Modules:
  0.0 33.9 jit_solution(3244100666410356506)
XLA Ops:
  0.0 0.0 copy-start.1
  0.0 0.0 copy-start
  0.0 2.0 %spectrum.1 = bf16[16,4,128]{2,1,0:T(4,128)(2,1)S(1)} custom-call(f32[128,2048]{1,0:T(8,128)} %gathers_ref.3, bf16[128,2048]{1,0:T(8,128)(2,1)} %constant.6.clone.table_ref), custom_call_target="tpu_custom_call" | custom-call | tf_op jit(solution)/shard_map/spectrum/spectrum/pallas_call | solution.py:260
  2.1 13.7 %all_to_all.10.incoming_ref = bf16[16,4,128]{2,1,0:T(4,128)(2,1)S(1)} all-to-all(bf16[16,4,128]{2,1,0:T(4,128)(2,1)S(1)} %spectrum.1), channel_id=1, replica_groups=mesh['survey'=2,'freq'=16] {'freq'}, dimensions={0} | all-to-all | bytes 32768 | tf_op jit(solution)/shard_map/all_to_all | solution.py:273
  15.7 7.4 %predict.1 = (bf16[16,4,256]{2,1,0:T(4,128)(2,1)S(1)}, f32[18,64,128]{2,1,0:T(8,128)S(1)}) custom-call(bf16[16,4,128]{2,1,0:T(4,128)(2,1)S(1)} %all_to_all.10.incoming_ref, s32[16]{0:T(128)} %tile_ref.1, s32[16]{0:T(128)} %slice_ref.1, f32[9,4,31]{2,1,0:T(4,128)} %bitcast.3, f32[4,128,31]{2,1,0:T(8,128)} %constant.7.clone.lag_ref, ...), custom_call_target="tpu_custom_call" | custom-call | tf_op jit(solution)/shard_map/predict/predict/pallas_call | solution.py:277
  23.2 9.2 %all_to_all.11.returned_ref = bf16[16,4,256]{2,1,0:T(4,128)(2,1)S(1)} all-to-all(bf16[16,4,256]{2,1,0:T(4,128)(2,1)S(1)} %get-tuple-element.7), channel_id=1, replica_groups=mesh['survey'=2,'freq'=16] {'freq'}, dimensions={0} | all-to-all | bytes 65536 | tf_op jit(solution)/shard_map/all_to_all | solution.py:306
  32.4 0.0 copy-done.1
  32.4 0.0 copy-done
  32.4 1.5 %subtract.1 = f32[128,2048]{1,0:T(8,128)} custom-call(bf16[16,4,256]{2,1,0:T(4,128)(2,1)S(1)} %all_to_all.11.returned_ref, f32[18,64,128]{2,1,0:T(8,128)S(1)} %get-tuple-element.8.coefficient_ref, bf16[192,2048]{1,0:T(8,128)(2,1)S(1)} %copy-done.1, f32[128,2048]{1,0:T(8,128)S(1)} %copy-done), custom_call_target="tpu_custom_call" | custom-call | tf_op jit(solution)/shard_map/subtract/subtract/pallas_call | solution.py:308
Async XLA Ops:
  0.0 32.4 %copy-start.1 = (bf16[192,2048]{1,0:T(8,128)(2,1)S(1)}, bf16[192,2048]{1,0:T(8,128)(2,1)}, u32[]{:S(2)}) copy-start(bf16[192,2048]{1,0:T(8,128)(2,1)} %constant.8.clone.table_ref) | copy-start | bytes 2359300
  0.0 32.4 %copy-start = (f32[128,2048]{1,0:T(8,128)S(1)}, f32[128,2048]{1,0:T(8,128)}, u32[]{:S(2)}) copy-start(f32[128,2048]{1,0:T(8,128)} %gathers_ref.3) | copy-start | bytes 3145732
where the time goes:
time: 34.1 us; the launch traced here: 33.9 us
  blocking collectives  22.9 us (67%)
  Pallas kernels  11 us (32%)
    all_to_all x1, blocking collectives, local(): lax.all_to_all(outgoing, 'freq', split_axis=0, concat_axis=0, tiled=True)  13.7 us
    all_to_all x1, blocking collectives, local(): lax.all_to_all(sending, 'freq', split_axis=0, concat_axis=0, tiled=True)  9.2 us
    pallas_call x1, Pallas kernels, local(): pl.pallas_call(functools.partial(predict_kernel, kept_bins, pieces), out_...  7.42 us
    pallas_call x1, Pallas kernels, local(): pl.pallas_call(functools.partial(spectrum_kernel, chunk), out_shape=jax.S...  2.05 us
    pallas_call x1, Pallas kernels, local(): pl.pallas_call(functools.partial(subtract_kernel, chunk), out_shape=jax.S...  1.5 us

commit v1 on v0

--- a/solution.py
+++ b/solution.py
@@ -12,6 +12,7 @@
 
 FIRST = 40
 REACH = 4
+IN_FLIGHT = 2
 VMEM_LIMIT = 40 * 1024 * 1024
 
 
@@ -67,7 +68,7 @@
                 pltpu.make_async_copy(table_ref.at[:, part], table.at[:, part], sems.at[1, step]),
             )
         )
-    for pair in copies:
+    for pair in copies[:IN_FLIGHT]:
         for copy in pair:
             copy.start()
     dot = functools.partial(
@@ -79,6 +80,8 @@
     for step, pair in enumerate(copies):
         for copy in pair:
             copy.wait()
+        for copy in copies[step + IN_FLIGHT] if step + IN_FLIGHT < len(copies) else ():
+            copy.start()
         part = pl.ds(step * chunk, chunk)
         high, low = split_array(held[:, part])
         weights = table[:, part]
@@ -145,15 +148,25 @@
     ]
     for copy in small:
         copy.start()
-    copies = {}
-    for slot in range(slots):
-        for piece in range(pieces):
-            for part in range(2):
-                where = (slot, part, pl.ds(piece * span, span))
-                copies[slot, piece, part] = pltpu.make_async_copy(
-                    operator_ref.at[where], operator.at[where], sems.at[slot, piece, part]
-                )
-                copies[slot, piece, part].start()
+    order = [
+        (slot, part, pl.ds(piece * span, span))
+        for slot in range(slots)
+        for piece in range(pieces)
+        for part in range(2)
+    ]
+    copies = [
+        pltpu.make_async_copy(operator_ref.at[where], operator.at[where], sems.at[i])
+        for i, where in enumerate(order)
+    ]
+    for copy in copies[:IN_FLIGHT]:
+        copy.start()
+
+    def arrived(index):
+        copies[index].wait()
+        if index + IN_FLIGHT < len(copies):
+            copies[index + IN_FLIGHT].start()
+        return operator[order[index]]
+
     for copy in small:
         copy.wait()
     for k in range(devices):
@@ -173,11 +186,9 @@
     kept = {}
     for slot in range(slots):
         for piece in range(pieces):
-            where = pl.ds(piece * span, span)
-            copies[slot, piece, 0].wait()
-            by_real = dot(spectrum, operator[slot, 0, where])
-            copies[slot, piece, 1].wait()
-            by_imag = swap_pairs(dot(spectrum, operator[slot, 1, where]))
+            index = 2 * (slot * pieces + piece)
+            by_real = dot(spectrum, arrived(index))
+            by_imag = swap_pairs(dot(spectrum, arrived(index + 1)))
             product = jnp.where(row_ids % 2 == 0, by_real - by_imag, by_real + by_imag)
             if slot:
                 product = jnp.where(row_ids // 2 % slots == slot, product, kept[piece])
@@ -239,6 +250,19 @@
 
 def in_hbm(values):
     return pltpu.with_memory_space_constraint(values, pltpu.HBM)
+
+
+def exchange(chunks, devices):
+    inner = 1 << (devices.bit_length() - 1) // 2
+    outer = devices // inner
+    shape = chunks.shape[1:]
+    near = [[o * inner + i for i in range(inner)] for o in range(outer)]
+    far = [[o * inner + i for o in range(outer)] for i in range(inner)]
+    by_inner = jnp.swapaxes(chunks.reshape(outer, inner, *shape), 0, 1)
+    held = lax.all_to_all(by_inner, "freq", 0, 0, axis_index_groups=near, tiled=True)
+    by_outer = jnp.swapaxes(held, 0, 1)
+    came = lax.all_to_all(by_outer, "freq", 0, 0, axis_index_groups=far, tiled=True)
+    return came.reshape(devices, *shape)
 
 
 def local(gathers, operator, filters, tile_of, slice_len):
@@ -270,7 +294,7 @@
             compiler_params=params,
             name="spectrum",
         )(in_hbm(gathers), in_hbm(jnp.asarray(forward_table)))
-    incoming = lax.all_to_all(outgoing, "freq", split_axis=0, concat_axis=0, tiled=True)
+    incoming = exchange(outgoing, devices)
     with jax.named_scope("predict"):
         tables = lag_tables(band_bins, lags, length)
         pieces = 2
@@ -291,7 +315,7 @@
                 pltpu.VMEM((devices, group_rows, traces), jnp.float32),
                 pltpu.VMEM((devices, group_rows, traces), jnp.float32),
                 pltpu.SemaphoreType.DMA((4,)),
-                pltpu.SemaphoreType.DMA((slots, pieces, 2)),
+                pltpu.SemaphoreType.DMA((slots * pieces * 2,)),
             ],
             compiler_params=params,
             name="predict",
@@ -303,7 +327,7 @@
             in_hbm(jnp.asarray(tables)),
             in_hbm(operator),
         )
-    returned = lax.all_to_all(sending, "freq", split_axis=0, concat_axis=0, tiled=True)
+    returned = exchange(sending, devices)
     with jax.named_scope("subtract"):
         return pl.pallas_call(
             functools.partial(subtract_kernel, chunk),

time: 34.1 us -> 44.3 us (1.30)
  blocking collectives: 22.9 us -> 32.5 us
    all_to_all x2 -> x4, blocking collectives: 22.9 us -> 32.5 us  [the longest x2 18.3 us: exchange(): lax.all_to_all(by_outer, 'freq', 0, 0, axis_index_groups=far, tiled=True)]
    pallas_call x1, Pallas kernels: 2.05 us -> 2.63 us  [local(): pl.pallas_call(functools.partial(spectrum_kernel, chunk), out_shape=jax.S...]
where the time goes in v1:
time: 44.3 us; the launch traced here: 43.8 us
  blocking collectives  32.5 us (73%)
  Pallas kernels  11.3 us (26%)
    all_to_all x2, blocking collectives, exchange(): lax.all_to_all(by_outer, 'freq', 0, 0, axis_index_groups=far, tiled=True)  18.3 us
    all_to_all x2, blocking collectives, exchange(): lax.all_to_all(by_inner, 'freq', 0, 0, axis_index_groups=near, tiled=True)  14.2 us
    pallas_call x1, Pallas kernels, local(): pl.pallas_call(functools.partial(predict_kernel, kept_bins, pieces), out_...  7.13 us
    pallas_call x1, Pallas kernels, local(): pl.pallas_call(functools.partial(spectrum_kernel, chunk), out_shape=jax.S...  2.63 us
    pallas_call x1, Pallas kernels, local(): pl.pallas_call(functools.partial(subtract_kernel, chunk), out_shape=jax.S...  1.5 us

profile of v1, /device:TPU:0, one launch (start us, length us, event | category | flops | bytes accessed | tf_op | source)
XLA Modules:
  0.0 43.8 jit_solution(2728651386380724916)
XLA Ops:
  0.0 0.0 copy-start.1
  0.0 0.0 copy-start
  0.0 2.6 %spectrum.1 = bf16[16,4,128]{2,1,0:T(4,128)(2,1)S(1)} custom-call(f32[128,2048]{1,0:T(8,128)} %gathers_ref.3, bf16[128,2048]{1,0:T(8,128)(2,1)} %constant.6.clone.table_ref), custom_call_target="tpu_custom_call" | custom-call | tf_op jit(solution)/shard_map/spectrum/spectrum/pallas_call | solution.py:284
  2.7 7.9 %all_to_all.20 = bf16[4,4,4,128]{3,2,1,0:T(4,128)(2,1)S(1)} all-to-all(bf16[4,4,4,128]{3,2,1,0:T(4,128)(2,1)S(1)} %bitcast.21), channel_id=1, replica_groups={{0,1,2,3},{4,5,6,7},{8,9,10,11},{12,13,14,15},{16,17,18,19},{20,21,22,2..., dimensions={0} | all-to-all | bytes 32768 | tf_op jit(solution)/shard_map/all_to_all | solution.py:262
  10.6 10.3 %all_to_all.21 = bf16[4,4,4,128]{3,2,1,0:T(4,128)(2,1)S(1)} all-to-all(bf16[4,4,4,128]{3,2,1,0:T(4,128)(2,1)S(1)} %copy.14), channel_id=1, replica_groups={{0,4,8,12},{1,5,9,13},{2,6,10,14},{3,7,11,15},{16,20,24,28},{17,21,25,2..., dimensions={0} | all-to-all | bytes 32768 | tf_op jit(solution)/shard_map/all_to_all | solution.py:264
  20.9 7.1 %predict.1 = (bf16[16,4,256]{2,1,0:T(4,128)(2,1)S(1)}, f32[18,64,128]{2,1,0:T(8,128)S(1)}) custom-call(bf16[16,4,128]{2,1,0:T(4,128)(2,1)S(1)} %bitcast.16, s32[16]{0:T(128)} %tile_ref.1, s32[16]{0:T(128)} %slice_ref.1, f32[9,4,31]{2,1,0:T(4,128)} %bitcast.23, f32[4,128,31]{2,1,0:T(8,128)} %constant.7.clone.lag_ref, bf16[2,2,1024,1024]{3,2,1,0:T(8,128)(2,1)} %operator_ref.1), custom_call_target="tpu_custom_call" | custom-call | tf_op jit(solution)/shard_map/predict/predict/pallas_call | solution.py:301
  28.0 6.3 %all_to_all.22 = bf16[4,4,4,256]{3,2,1,0:T(4,128)(2,1)S(1)} all-to-all(bf16[4,4,4,256]{3,2,1,0:T(4,128)(2,1)S(1)} %bitcast.19), channel_id=1, replica_groups={{0,1,2,3},{4,5,6,7},{8,9,10,11},{12,13,14,15},{16,17,18,19},{20,21,22,2..., dimensions={0} | all-to-all | bytes 65536 | tf_op jit(solution)/shard_map/all_to_all | solution.py:262
  34.3 8.0 %all_to_all.23 = bf16[4,4,4,256]{3,2,1,0:T(4,128)(2,1)S(1)} all-to-all(bf16[4,4,4,256]{3,2,1,0:T(4,128)(2,1)S(1)} %copy.16), channel_id=1, replica_groups={{0,4,8,12},{1,5,9,13},{2,6,10,14},{3,7,11,15},{16,20,24,28},{17,21,25,2..., dimensions={0} | all-to-all | bytes 65536 | tf_op jit(solution)/shard_map/all_to_all | solution.py:264
  42.3 0.0 copy-done.1
  42.3 0.0 copy-done
  42.3 1.5 %subtract.1 = f32[128,2048]{1,0:T(8,128)} custom-call(bf16[16,4,256]{2,1,0:T(4,128)(2,1)S(1)} %bitcast.15, f32[18,64,128]{2,1,0:T(8,128)S(1)} %get-tuple-element.8.coefficient_ref, bf16[192,2048]{1,0:T(8,128)(2,1)S(1)} %copy-done.1, f32[128,2048]{1,0:T(8,128)S(1)} %copy-done), custom_call_target="tpu_custom_call" | custom-call | tf_op jit(solution)/shard_map/subtract/subtract/pallas_call | solution.py:332
  (4 shorter events, 0.0 us)
Async XLA Ops:
  0.0 42.3 %copy-start.1 = (bf16[192,2048]{1,0:T(8,128)(2,1)S(1)}, bf16[192,2048]{1,0:T(8,128)(2,1)}, u32[]{:S(2)}) copy-start(bf16[192,2048]{1,0:T(8,128)(2,1)} %constant.8.clone.table_ref) | copy-start | bytes 2359300
  0.0 42.3 %copy-start = (f32[128,2048]{1,0:T(8,128)S(1)}, f32[128,2048]{1,0:T(8,128)}, u32[]{:S(2)}) copy-start(f32[128,2048]{1,0:T(8,128)} %gathers_ref.3) | copy-start | bytes 3145732
